TPU v7x, 256 devices: a whole 4x4x8 slice. The times are simulated.
256 devices in a mesh: cores: 4 (over x), mode: 64 (over z, y, core).
Axes of the slice: x: 4, y: 4, z: 8, core: 2. Of those that a mesh axis runs over, the one named last changes fastest.
Arguments:
- x_cores: bfloat16 [4, 512, 1024, 512], P('cores', None, 'mode'), may hold values from -0.25 to 0.25
- y_cores: bfloat16 [4, 256, 1024, 256], P('cores', None, 'mode'), may hold values from -40 to 40
- left_boundary: bfloat16 [256, 512], replicated, may hold values from -6 to 6
- right_boundary: bfloat16 [256, 512], replicated, may hold values from -6 to 6
Outputs:
- projected: bfloat16 [4, 256, 1024, 256], P('cores', None, 'mode')
All inputs are finite; a program needn't handle non-finite values.
Results may differ from a plain program's by a relative error of at most 0.014.
Values may be sent and summed in bfloat16 or wider, within the bound.
No kernel may reach another device: no remote copies, remote signals or barrier semaphores. Data moves between devices by JAX's collectives and lax.ppermute only.
A program may use at most 128 MiB of HBM per device.

v0:
```python
import functools
import math

import jax
import jax.numpy as jnp
from jax import lax
from jax.experimental import pallas as pl
from jax.experimental.pallas import tpu as pltpu
from jax.sharding import PartitionSpec as P

EPSILON = 1e-06
TILES = 8
PARTS = 4
LANES = 128
VMEM_LIMIT = 36 * 1024 * 1024
BF16 = jnp.bfloat16
F32 = jnp.float32
NT = (((1,), (1,)), ((), ()))
TN = (((0,), (0,)), ((), ()))
SMEM, VMEM, HBM = pltpu.SMEM, pltpu.VMEM, pltpu.HBM
IDLE, LEFT, RIGHT, APPLY = 0, 1, 2, 3


def unpack(e_ref, env_ref):
    chunks, rows, width = e_ref.shape
    lanes = env_ref.shape[1] // width
    for j in range(chunks):
        r, k = j // lanes, j % lanes
        env_ref[rows * r : rows * (r + 1), width * k : width * (k + 1)] = e_ref[j]


def hand_out(acc, scale, core, kept, given):
    chunks, rows, width = kept.shape
    lanes = acc.shape[1] // width
    half = acc.shape[0] // 2
    for ref, owner in ((given, 1 - core), (kept, core)):
        start = pl.multiple_of(owner * half, half)
        for j in range(chunks):
            r, k = j // lanes, j % lanes
            value = acc[pl.ds(start + rows * r, rows), width * k : width * (k + 1)]
            if scale is not None:
                value = value * scale
            ref[j] = value.astype(BF16)


def scale_of(env):
    wide = env.astype(F32)
    return lax.rsqrt(jnp.mean(wide * wide) + EPSILON)


def tile_copies(x_ref, x_buf, sems):
    return [tile_copy(x_ref, x_buf, sems, t) for t in range(TILES)]


def tile_copy(x_ref, x_buf, sems, t):
    rows = x_buf.shape[0] // TILES
    part = block_of(t, rows)
    return pltpu.make_async_copy(x_ref.at[part], x_buf.at[part], sems.at[t])


def block_of(t, size):
    return pl.ds(t * size if isinstance(t, int) else pl.multiple_of(t * size, size), size)


def begin(copies):
    for copy in copies:
        copy.start()


def mode_major(y_buf, y2, points):
    step = y2.shape[0] // TILES

    @pl.loop(0, TILES)
    def _(t):
        y2[block_of(t, step), :] = y_buf[block_of(t, step * points), :].reshape(step, y2.shape[1])


def left_sum(env, x_ref, x, sems, y2, w, acc):
    width = env.shape[0]
    turned = env.T

    @pl.loop(0, y2.shape[1] // (2 * width))
    def _(i):
        lanes = block_of(i, 2 * width)
        w[:, lanes] = jnp.dot(turned, y2[:, lanes], preferred_element_type=F32).astype(BF16)

    rows = x.shape[0] // PARTS
    ranks = w.shape[0] // PARTS

    def term(t):
        for tile in range(TILES // PARTS):
            tile_copy(x_ref, x, sems, t * (TILES // PARTS) + tile).wait()
        own = w[block_of(t, ranks), :].reshape(rows, width)
        return lax.dot_general(own, x[block_of(t, rows), :], TN, preferred_element_type=F32)

    acc[...] = jnp.zeros_like(acc)

    @pl.loop(0, PARTS)
    def _(t):
        acc[...] += term(t)


def carry_back(env, x_ref, x, sems, natural, cb, cb_out, store_sems):
    rows = x.shape[0] // TILES
    ranks = cb.shape[0] // TILES
    turned = env.T

    @pl.loop(0, TILES)
    def _(t):
        tile_copy(x_ref, x, sems, t).wait()
        value = jnp.dot(x[block_of(t, rows), :], turned, preferred_element_type=F32)
        natural[...] = value.astype(BF16)
        cb[block_of(t, ranks), :] = natural[...].reshape(ranks, cb.shape[1])
        tile_copy(cb, cb_out, store_sems, t).start()


def right_sum(y2, cb, acc):
    half = cb.shape[0] // 2

    @pl.loop(0, 2)
    def _(n):
        acc[:, block_of(n, half)] = lax.dot_general(
            y2[...], cb[block_of(n, half), :], NT, preferred_element_type=F32
        )


def apply(env, x_ref, x, sems, xt, narrow, applied):
    source_rank = env.shape[1]
    rows = x.shape[0] // TILES
    ranks = xt.shape[0] // TILES

    @pl.loop(0, TILES)
    def _(t):
        tile_copy(x_ref, x, sems, t).wait()
        xt[block_of(t, ranks), :] = x[block_of(t, rows), :].reshape(ranks, xt.shape[1])

    @pl.loop(0, xt.shape[1] // source_rank)
    def _(i):
        lanes = block_of(i, source_rank)
        narrow[:, lanes] = jnp.dot(env, xt[:, lanes], preferred_element_type=F32).astype(BF16)

    blocks = applied.shape[1] // source_rank
    own = env.shape[0] // blocks

    @pl.loop(0, blocks)
    def _(j):
        applied[:, block_of(j, source_rank)] = narrow[block_of(j, own), :].reshape(source_rank, source_rank)


def first_kernel(
    points, role, lb, rb, x, y, kept, given, cb_out, y2, x_buf, y_buf, cb, w, natural, acc, env_buf, sems, store_sems, side
):
    load_y = pltpu.make_async_copy(y, y_buf, side.at[0])
    stores = tile_copies(cb, cb_out, store_sems)
    copies = tile_copies(x, x_buf, sems)

    @pl.when(role[0] == IDLE)
    def _():
        load_y.start()
        load_y.wait()
        mode_major(y_buf, y2, points)
        kept[...] = jnp.zeros_like(kept)
        given[...] = jnp.zeros_like(given)

    @pl.when(role[0] == LEFT)
    def _():
        load_y.start()
        load_env = pltpu.make_async_copy(lb, env_buf, side.at[2])
        load_env.start()
        load_y.wait()
        begin(copies)
        mode_major(y_buf, y2, points)
        load_env.wait()
        left_sum(env_buf[...], x, x_buf, sems, y2, w, acc)
        hand_out(acc, None, role[1], kept, given)

    @pl.when(role[0] == RIGHT)
    def _():
        load_env = pltpu.make_async_copy(rb, env_buf, side.at[2])
        load_env.start()
        load_y.start()
        begin(copies)
        load_env.wait()
        carry_back(env_buf[...], x, x_buf, sems, natural, cb, cb_out, store_sems)
        load_y.wait()
        mode_major(y_buf, y2, points)
        right_sum(y2, cb, acc)
        hand_out(acc, None, role[1], kept, given)
        for store in stores:
            store.wait()


def next_kernel(
    role, e, lb, x, y2, kept, given, cb_out, x_buf, cb, w, natural, xt, narrow, acc, env_buf, sems, store_sems, side
):
    stores = tile_copies(cb, cb_out, store_sems)
    copies = tile_copies(x, x_buf, sems)

    @pl.when(role[0] == IDLE)
    def _():
        kept[...] = jnp.zeros_like(kept)
        given[...] = jnp.zeros_like(given)

    @pl.when(role[0] == APPLY)
    def _():
        kept[...] = jnp.zeros_like(kept)
        given[...] = jnp.zeros_like(given)
        load_env = pltpu.make_async_copy(lb, env_buf, side.at[0])
        load_env.start()
        begin(copies)
        load_env.wait()
        apply(env_buf[...], x, x_buf, sems, xt, narrow, cb)
        for store in stores:
            store.start()
        for store in stores:
            store.wait()

    @pl.when(role[0] == LEFT)
    def _():
        begin(copies)
        unpack(e, env_buf)
        env = env_buf[...]
        left_sum(env, x, x_buf, sems, y2, w, acc)
        hand_out(acc, scale_of(env), role[1], kept, given)

    @pl.when(role[0] == RIGHT)
    def _():
        begin(copies)
        unpack(e, env_buf)
        env = env_buf[...]
        carry_back(env, x, x_buf, sems, natural, cb, cb_out, store_sems)
        right_sum(y2, cb, acc)
        hand_out(acc, scale_of(env), role[1], kept, given)
        for store in stores:
            store.wait()


def last_kernel(role, e1, e2, e3, cb0, cb1, cb2, out, cb, out_buf, narrow, env_buf, factor, sems, side):
    target_rank, source_rank = env_buf.shape
    block = out_buf.shape[0] // TILES
    lanes = cb.shape[1] // TILES

    def load(source, j):
        part = block_of(j, lanes)
        return pltpu.make_async_copy(source.at[:, part], cb.at[:, part], side.at[j])

    def store(t):
        part = block_of(t, block)
        return pltpu.make_async_copy(out_buf.at[part], out.at[part], sems.at[t])

    for group, source in ((0, cb1), (1, cb2), (2, cb1), (3, cb0)):

        @pl.when(role[0] == group)
        def _():
            for j in range(TILES):
                load(source, j).start()

    for group, e in ((1, e1), (2, e2)):

        @pl.when(role[0] == group)
        def _():
            unpack(e, env_buf)

    @pl.when((role[0] == 0) | (role[0] == 3))
    def _():
        unpack(e3, env_buf)

    other = jnp.where(role[0] == 1, scale_of(e2[...]), scale_of(e1[...]))
    inner = (role[0] == 1) | (role[0] == 2)
    env = env_buf[...]
    factor[0] = scale_of(env) * jnp.where(inner, other, 1.0) * (1.0 / math.sqrt(source_rank))

    @pl.when(role[0] == 0)
    def _():
        @pl.loop(0, TILES)
        def _(t):
            load(cb1, t).wait()
            value = lax.dot_general(cb[:, block_of(t, lanes)], env_buf[...], NT, preferred_element_type=F32)
            out_buf[block_of(t, block), :] = (value * factor[0]).astype(BF16)
            store(t).start()

    @pl.when(role[0] != 0)
    def _():
        @pl.loop(0, TILES)
        def _(j):
            load(cb1, j).wait()
            part = block_of(j, lanes)
            value = jnp.dot(env_buf[...], cb[:, part], preferred_element_type=F32)
            narrow[:, part] = (value * factor[0]).astype(BF16)

        @pl.loop(0, TILES)
        def _(t):
            own = narrow[block_of(t, target_rank // TILES), :]
            out_buf[block_of(t, block), :] = own.reshape(block, target_rank)
            store(t).start()

    for t in range(TILES):
        store(t).wait()


def place(kind):
    return pl.BlockSpec(memory_space=kind)


def in_hbm(array):
    return pltpu.with_memory_space_constraint(array, HBM)


def step_calls(points, target_rank, source_rank):
    chunk = (32, target_rank * source_rank // (64 * LANES), LANES)
    rows = source_rank * points
    flat = points * target_rank
    s_shape = jax.ShapeDtypeStruct(chunk, BF16)
    cb_shape = jax.ShapeDtypeStruct((source_rank, flat), BF16)
    y2_shape = jax.ShapeDtypeStruct((target_rank, flat), BF16)
    x_buf = pltpu.VMEM((rows, source_rank), BF16)
    cb = pltpu.VMEM(cb_shape.shape, BF16)
    y_buf = pltpu.VMEM((target_rank * points, target_rank), BF16)
    w = pltpu.VMEM(cb_shape.shape, BF16)
    natural = pltpu.VMEM((rows // TILES, target_rank), BF16)
    xt = pltpu.VMEM((source_rank, points * source_rank), BF16)
    wide = pltpu.VMEM((target_rank, points * source_rank), BF16)
    narrow = pltpu.VMEM((target_rank, flat), BF16)
    acc = pltpu.VMEM((target_rank, source_rank), F32)
    env_buf = pltpu.VMEM((target_rank, source_rank), BF16)
    sems = pltpu.SemaphoreType.DMA((TILES,))
    side = pltpu.SemaphoreType.DMA((3,))
    params = pltpu.CompilerParams(vmem_limit_bytes=VMEM_LIMIT)
    first = pl.pallas_call(
        functools.partial(first_kernel, points),
        out_shape=(s_shape, s_shape, HBM(cb_shape.shape, BF16), y2_shape),
        in_specs=[place(SMEM)] + [place(HBM)] * 4,
        out_specs=(place(VMEM), place(VMEM), place(HBM), place(VMEM)),
        scratch_shapes=[x_buf, y_buf, cb, w, natural, acc, env_buf, sems, sems, side],
        compiler_params=params,
        name="first_step",
    )
    following = pl.pallas_call(
        next_kernel,
        out_shape=(s_shape, s_shape, HBM(cb_shape.shape, BF16)),
        in_specs=[place(SMEM), place(VMEM), place(HBM), place(HBM), place(VMEM)],
        out_specs=(place(VMEM), place(VMEM), place(HBM)),
        scratch_shapes=[x_buf, cb, w, natural, xt, wide, acc, env_buf, sems, sems, side],
        compiler_params=params,
        name="next_step",
    )
    last = pl.pallas_call(
        last_kernel,
        out_shape=jax.ShapeDtypeStruct((target_rank * points, target_rank), BF16),
        in_specs=[place(SMEM)] + [place(VMEM)] * 3 + [place(HBM)] * 3,
        out_specs=place(HBM),
        scratch_shapes=[cb, y_buf, narrow, env_buf, pltpu.SMEM((1,), F32), sems, sems],
        compiler_params=params,
        name="projection",
    )
    return first, following, last


def exchange(kept, given, route):
    chunks, rows, width = kept.shape
    devices = lax.axis_size("mode")
    same_core = [list(range(c, devices, 2)) for c in range(2)]
    same_chip = [[d, d + 1] for d in range(0, devices, 2)]
    taken = lax.ppermute(given, "mode", [(d, d ^ 1) for d in range(devices)])
    chip = (kept.astype(F32) + taken.astype(F32)).astype(BF16)
    mine = lax.all_to_all(chip, "mode", 0, 0, axis_index_groups=same_core, tiled=True)
    summed = jnp.sum(mine.astype(F32), axis=0).astype(BF16)
    summed = lax.ppermute(summed, "cores", route)
    copies = jnp.broadcast_to(summed[None], (chunks, rows, width))
    whole = lax.all_to_all(copies, "mode", 0, 0, axis_index_groups=same_core, tiled=True)
    whole = lax.all_gather(whole, "mode", axis_index_groups=same_chip)
    return whole.reshape(2 * chunks, rows, width)


def body(x_cores, y_cores, left_boundary, right_boundary):
    _, source_rank, points, _ = x_cores.shape
    target_rank = left_boundary.shape[0]
    group = lax.axis_index("cores")
    core = lax.axis_index("mode") % 2
    x = in_hbm(x_cores.reshape(source_rank * points, source_rank))
    y = in_hbm(y_cores.reshape(target_rank * points, target_rank))
    left_boundary, right_boundary = in_hbm(left_boundary), in_hbm(right_boundary)
    first, following, last = step_calls(points, target_rank, source_rank)

    def role_at(position):
        role = jnp.where(group == position, LEFT, jnp.where(group == 3 - position, RIGHT, IDLE))
        if position == 1:
            role = jnp.where(group == 0, APPLY, role)
        return jnp.stack([role, core]).astype(jnp.int32)

    kept, given, cb, y2 = first(role_at(0), left_boundary, right_boundary, x, y)
    carried = [cb]
    envs = [exchange(kept, given, [(0, 1), (3, 2)])]
    for position, route in ((1, [(1, 2), (2, 1)]), (2, [(2, 3), (1, 0)])):
        kept, given, cb = following(role_at(position), envs[-1], left_boundary, x, y2)
        carried.append(cb)
        envs.append(exchange(kept, given, route))
    out = last(group.astype(jnp.int32).reshape(1), *envs, *map(in_hbm, carried))
    return out.reshape(1, target_rank, points, target_rank)


def solution(mesh):
    in_specs = (P("cores", None, "mode", None), P("cores", None, "mode", None), P(), P())
    out_specs = P("cores", None, "mode", None)
    return jax.shard_map(body, mesh=mesh, in_specs=in_specs, out_specs=out_specs, check_vma=False)
```

profile of v0, /device:TPU:6, one launch (start us, length us, event | category | flops | bytes accessed | tf_op | source)
XLA Modules:
  0.0 147.8 jit_solution(14367369504562276534)
XLA Ops:
  0.0 0.1 pad_add_fusion.role
  0.1 9.6 %first_step.1 = (bf16[32,16,128]{2,1,0:T(8,128)(2,1)S(1)}, bf16[32,16,128]{2,1,0:T(8,128)(2,1)S(1)}, bf16[512,4096]{1,0:T(8,128)(2,1)}, bf16[256,4096]{1,0:T(8,128)(2,1)S(1)}) custom-call(s32[2]{0:T(128)S(1)} %pad_add_fusion.role, bf16[256,512]{1,0:T(8,128)(2,1)} %lb.5, bf16[256,512]{1,0:T(8,128)(2,1)} %rb.1, bf16[8192,512]{1,0:T(8,128)(2,1)} %bitcast.8, ...), custom_call_target="tpu_custom_call" | custom-call | tf_op jit(solution)/shard_map/first_step/pallas_call | solution.py:391
  9.7 0.1 collective-permute-start
  9.8 1.3 collective-permute-done
  11.2 22.1 %all_to_all.30 = bf16[32,16,128]{2,1,0:T(8,128)(2,1)S(1)} all-to-all(bf16[32,16,128]{2,1,0:T(8,128)(2,1)S(1)} %add_convert_fusion.2), channel_id=1, replica_groups={{0,2,4,6,8,10,12,14,16,18,20,22,24,26,28,30,32,34,36,38,40,42,44,46,48,..., dimensions={0} | all-to-all | bytes 262144 | tf_op jit(solution)/shard_map/all_to_all | solution.py:366
  33.3 1.3 collective-permute-start.1
  34.6 1.3 collective-permute-done.1
  35.9 0.7 broadcast_in_dim.6
  36.6 3.9 %all-to-all-start.1 = ((bf16[32,16,128]{2,1,0:T(8,128)(2,1)}), bf16[32,16,128]{2,1,0:T(8,128)(2,1)S(1)}, u32[]{:S(2)}, u32[]{:S(2)}) async-start(bf16[32,16,128]{2,1,0:T(8,128)(2,1)} %broadcast_in_dim.6), calls=%async_computation.1 | async-start | bytes 262144 | tf_op jit(solution)/shard_map/all_to_all | solution.py:370
  40.5 0.1 pad_add_fusion.1.role
  40.6 10.5 %all-to-all-done.1 = bf16[32,16,128]{2,1,0:T(8,128)(2,1)S(1)} async-done(((bf16[32,16,128]{2,1,0:T(8,128)(2,1)}), bf16[32,16,128]{2,1,0:T(8,128)(2,1)S(1)}, u32[]{:S(2)}, u32[]{:S(2)}) %all-to-all-start.1) | async-done | bytes 131104 | tf_op jit(solution)/shard_map/all_to_all | solution.py:370
  51.0 2.0 %all-gather.e.e1 = bf16[64,16,128]{2,1,0:T(8,128)(2,1)S(1)} all-gather(bf16[32,16,128]{2,1,0:T(8,128)(2,1)S(1)} %all-to-all-done.1), channel_id=2, replica_groups={{0,1},{2,3},{4,5},{6,7},{8,9},{10,11},{12,13},{14,15},{16,17},{18,19},{..., dimensions={0}, use_global_device_ids=true | all-gather | bytes 393216 | tf_op jit(solution)/shard_map/all_gather | solution.py:371
  53.0 0.8 next_step.2
  53.8 0.2 collective-permute-start.2
  54.0 1.2 collective-permute-done.2
  55.3 14.0 %all_to_all.31 = bf16[32,16,128]{2,1,0:T(8,128)(2,1)S(1)} all-to-all(bf16[32,16,128]{2,1,0:T(8,128)(2,1)S(1)} %add_convert_fusion.1), channel_id=1, replica_groups={{0,2,4,6,8,10,12,14,16,18,20,22,24,26,28,30,32,34,36,38,40,42,44,46,48,..., dimensions={0} | all-to-all | bytes 262144 | tf_op jit(solution)/shard_map/all_to_all | solution.py:366
  69.3 0.7 collective-permute-start.3
  70.0 0.0 collective-permute-done.3
  70.0 0.7 broadcast_in_dim.7
  70.7 3.9 %all-to-all-start.3 = ((bf16[32,16,128]{2,1,0:T(8,128)(2,1)}), bf16[32,16,128]{2,1,0:T(8,128)(2,1)S(1)}, u32[]{:S(2)}, u32[]{:S(2)}) async-start(bf16[32,16,128]{2,1,0:T(8,128)(2,1)} %broadcast_in_dim.7), calls=%async_computation.3 | async-start | bytes 262144 | tf_op jit(solution)/shard_map/all_to_all | solution.py:370
  74.6 0.1 pad_add_fusion.2.role
  74.6 10.5 %all-to-all-done.3 = bf16[32,16,128]{2,1,0:T(8,128)(2,1)S(1)} async-done(((bf16[32,16,128]{2,1,0:T(8,128)(2,1)}), bf16[32,16,128]{2,1,0:T(8,128)(2,1)S(1)}, u32[]{:S(2)}, u32[]{:S(2)}) %all-to-all-start.3) | async-done | bytes 131104 | tf_op jit(solution)/shard_map/all_to_all | solution.py:370
  85.1 2.0 %all-gather.1.e.e2 = bf16[64,16,128]{2,1,0:T(8,128)(2,1)S(1)} all-gather(bf16[32,16,128]{2,1,0:T(8,128)(2,1)S(1)} %all-to-all-done.3), channel_id=3, replica_groups={{0,1},{2,3},{4,5},{6,7},{8,9},{10,11},{12,13},{14,15},{16,17},{18,19},{..., dimensions={0}, use_global_device_ids=true | all-gather | bytes 393216 | tf_op jit(solution)/shard_map/all_gather | solution.py:371
  87.1 1.0 next_step.3
  88.1 0.2 collective-permute-start.4
  88.3 1.2 collective-permute-done.4
  89.6 14.1 %all_to_all.32 = bf16[32,16,128]{2,1,0:T(8,128)(2,1)S(1)} all-to-all(bf16[32,16,128]{2,1,0:T(8,128)(2,1)S(1)} %add_convert_fusion), channel_id=1, replica_groups={{0,2,4,6,8,10,12,14,16,18,20,22,24,26,28,30,32,34,36,38,40,42,44,46,48,..., dimensions={0} | all-to-all | bytes 262144 | tf_op jit(solution)/shard_map/all_to_all | solution.py:366
  103.7 1.3 collective-permute-start.5
  105.0 21.6 %collective-permute-done.5 = bf16[16,128]{1,0:T(8,128)(2,1)S(1)} collective-permute-done((bf16[16,128]{1,0:T(8,128)(2,1)S(1)}, bf16[16,128]{1,0:T(8,128)(2,1)S(1)}, u32[]{:S(2)}, u32[]{:S(2)}) %collective-permute-start.5) | collective-permute-done | bytes 4128 | tf_op jit(solution)/shard_map/ppermute | solution.py:368
  126.7 13.8 %all_to_all.33 = bf16[32,16,128]{2,1,0:T(8,128)(2,1)S(1)} all-to-all(bf16[32,16,128]{2,1,0:T(8,128)(2,1)S(1)} %broadcast_in_dim.8), channel_id=1, replica_groups={{0,2,4,6,8,10,12,14,16,18,20,22,24,26,28,30,32,34,36,38,40,42,44,46,48,..., dimensions={0} | all-to-all | bytes 262144 | tf_op jit(solution)/shard_map/all_to_all | solution.py:370
  140.5 2.0 %all-gather.2.e3 = bf16[64,16,128]{2,1,0:T(8,128)(2,1)S(1)} all-gather(bf16[32,16,128]{2,1,0:T(8,128)(2,1)S(1)} %all_to_all.33), channel_id=4, replica_groups={{0,1},{2,3},{4,5},{6,7},{8,9},{10,11},{12,13},{14,15},{16,17},{18,19},{..., dimensions={0}, use_global_device_ids=true | all-gather | bytes 393216 | tf_op jit(solution)/shard_map/all_gather | solution.py:371
  142.5 5.1 %projection.1 = bf16[4096,256]{1,0:T(8,128)(2,1)} custom-call(s32[1]{0:T(128)} %bitcast.role, bf16[64,16,128]{2,1,0:T(8,128)(2,1)S(1)} %all-gather.e.e1, bf16[64,16,128]{2,1,0:T(8,128)(2,1)S(1)} %all-gather.1.e.e2, bf16[64,16,128]{2,1,0:T(8,128)(2,1)S(1)} %all-gather.2.e3, bf16[512,4096]{1,0:T(8,128)(2,1)} %get-tuple-element.22.cb0, ...), custom_call_target="tpu_custom_call" | custom-call | tf_op jit(solution)/shard_map/projection/pallas_call | solution.py:398
  (7 shorter events, 0.2 us)
Async XLA Ops:
  9.7 1.4 collective-permute-start
  33.3 2.6 %collective-permute-start.1 = (bf16[16,128]{1,0:T(8,128)(2,1)S(1)}, bf16[16,128]{1,0:T(8,128)(2,1)S(1)}, u32[]{:S(2)}, u32[]{:S(2)}) collective-permute-start(bf16[16,128]{1,0:T(8,128)(2,1)S(1)} %reduce_sum.36), channel_id=1, source_target_pairs={{0,64},{192,128},{1,65},{193,129},{2,66},{194,130},{3,67},{195,131... | collective-permute-start | bytes 12296 | tf_op jit(solution)/shard_map/ppermute | solution.py:368
  36.6 14.4 %all-to-all-start.1 = ((bf16[32,16,128]{2,1,0:T(8,128)(2,1)}), bf16[32,16,128]{2,1,0:T(8,128)(2,1)S(1)}, u32[]{:S(2)}, u32[]{:S(2)}) async-start(bf16[32,16,128]{2,1,0:T(8,128)(2,1)} %broadcast_in_dim.6), calls=%async_computation.1 | async-start | bytes 262144 | tf_op jit(solution)/shard_map/all_to_all | solution.py:370
  53.8 1.4 collective-permute-start.2
  69.3 0.7 collective-permute-start.3
  70.7 14.5 %all-to-all-start.3 = ((bf16[32,16,128]{2,1,0:T(8,128)(2,1)}), bf16[32,16,128]{2,1,0:T(8,128)(2,1)S(1)}, u32[]{:S(2)}, u32[]{:S(2)}) async-start(bf16[32,16,128]{2,1,0:T(8,128)(2,1)} %broadcast_in_dim.7), calls=%async_computation.3 | async-start | bytes 262144 | tf_op jit(solution)/shard_map/all_to_all | solution.py:370
  88.1 1.4 collective-permute-start.4
  103.7 22.9 %collective-permute-start.5 = (bf16[16,128]{1,0:T(8,128)(2,1)S(1)}, bf16[16,128]{1,0:T(8,128)(2,1)S(1)}, u32[]{:S(2)}, u32[]{:S(2)}) collective-permute-start(bf16[16,128]{1,0:T(8,128)(2,1)S(1)} %reduce_sum.38), channel_id=1, source_target_pairs={{128,192},{64,0},{129,193},{65,1},{130,194},{66,2},{131,195},{67,3... | collective-permute-start | bytes 12296 | tf_op jit(solution)/shard_map/ppermute | solution.py:368
where the time goes:
time: 150 us; the launch traced here: 148 us
  blocking collectives  70 us (47%)
  waiting for transfers between devices  47.7 us (32%)
  Pallas kernels  16.5 us (11%)
  starting transfers between devices  11.5 us (8%)
    all_to_all x3, blocking collectives, exchange(): lax.all_to_all(chip, 'mode', 0, 0, axis_index_groups=same_core, tiled=True)  50.2 us
    ppermute x3, waiting for transfers between devices, exchange(): summed = lax.ppermute(summed, 'cores', route)  23 us
    all_to_all x2, waiting for transfers between devices, exchange(): lax.all_to_all(copies, 'mode', 0, 0, axis_index_groups=same_core, tiled=T...  21 us
    all_to_all x1, blocking collectives, exchange(): lax.all_to_all(copies, 'mode', 0, 0, axis_index_groups=same_core, tiled=T...  13.8 us
    pallas_call x1, Pallas kernels, body(): kept, given, cb, y2 = first(role_at(0), left_boundary, right_boundary, x, y)  9.65 us
    all_to_all x2, starting transfers between devices, exchange(): lax.all_to_all(copies, 'mode', 0, 0, axis_index_groups=same_core, tiled=T...  7.73 us
    all_gather x3, blocking collectives, exchange(): whole = lax.all_gather(whole, 'mode', axis_index_groups=same_chip)  5.94 us
    pallas_call x1, Pallas kernels, body(): out = last(group.astype(jnp.int32).reshape(1), *envs, *map(in_hbm, carried))  5.13 us
  transfers between devices with their start and end apart: 8, of which 7 were waited for; matrix products, arithmetic and copies ran while one was open for 0% of the time, Pallas kernels for 0%

commit v1 on v0

--- a/solution.py
+++ b/solution.py
@@ -10,7 +10,8 @@
 
 EPSILON = 1e-06
 TILES = 8
-PARTS = 4
+PARTS = 2
+WINDOW = 3
 LANES = 128
 VMEM_LIMIT = 36 * 1024 * 1024
 BF16 = jnp.bfloat16
@@ -21,12 +22,15 @@
 IDLE, LEFT, RIGHT, APPLY = 0, 1, 2, 3
 
 
-def unpack(e_ref, env_ref):
-    chunks, rows, width = e_ref.shape
+def unpack(own, others, core, env_ref):
+    chunks, rows, width = own.shape
     lanes = env_ref.shape[1] // width
-    for j in range(chunks):
-        r, k = j // lanes, j % lanes
-        env_ref[rows * r : rows * (r + 1), width * k : width * (k + 1)] = e_ref[j]
+    half = env_ref.shape[0] // 2
+    for ref, owner in ((own, core), (others, 1 - core)):
+        for j in range(chunks):
+            r, k = j // lanes, j % lanes
+            start = pl.multiple_of(owner * half + rows * r, rows)
+            env_ref[pl.ds(start, rows), width * k : width * (k + 1)] = ref[j]
 
 
 def hand_out(acc, scale, core, kept, given):
@@ -43,9 +47,9 @@
             ref[j] = value.astype(BF16)
 
 
-def scale_of(env):
-    wide = env.astype(F32)
-    return lax.rsqrt(jnp.mean(wide * wide) + EPSILON)
+def scale_of(*parts):
+    wide = [part.astype(F32) for part in parts]
+    return lax.rsqrt(sum(jnp.mean(value * value) for value in wide) / len(parts) + EPSILON)
 
 
 def tile_copies(x_ref, x_buf, sems):
@@ -100,7 +104,7 @@
         acc[...] += term(t)
 
 
-def carry_back(env, x_ref, x, sems, natural, cb, cb_out, store_sems):
+def carry_back(env, window, x_ref, x, sems, natural, cb, cb_out, store_sems):
     rows = x.shape[0] // TILES
     ranks = cb.shape[0] // TILES
     turned = env.T
@@ -108,6 +112,13 @@
     @pl.loop(0, TILES)
     def _(t):
         tile_copy(x_ref, x, sems, t).wait()
+
+        if window < TILES:
+
+            @pl.when(t + window < TILES)
+            def _():
+                tile_copy(x_ref, x, sems, t + window).start()
+
         value = jnp.dot(x[block_of(t, rows), :], turned, preferred_element_type=F32)
         natural[...] = value.astype(BF16)
         cb[block_of(t, ranks), :] = natural[...].reshape(ranks, cb.shape[1])
@@ -179,9 +190,9 @@
         load_env = pltpu.make_async_copy(rb, env_buf, side.at[2])
         load_env.start()
         load_y.start()
-        begin(copies)
+        begin(copies[:WINDOW])
         load_env.wait()
-        carry_back(env_buf[...], x, x_buf, sems, natural, cb, cb_out, store_sems)
+        carry_back(env_buf[...], WINDOW, x, x_buf, sems, natural, cb, cb_out, store_sems)
         load_y.wait()
         mode_major(y_buf, y2, points)
         right_sum(y2, cb, acc)
@@ -191,7 +202,7 @@
 
 
 def next_kernel(
-    role, e, lb, x, y2, kept, given, cb_out, x_buf, cb, w, natural, xt, narrow, acc, env_buf, sems, store_sems, side
+    role, e, f, lb, x, y2, kept, given, cb_out, x_buf, cb, w, natural, xt, narrow, acc, env_buf, sems, store_sems, side
 ):
     stores = tile_copies(cb, cb_out, store_sems)
     copies = tile_copies(x, x_buf, sems)
@@ -218,7 +229,7 @@
     @pl.when(role[0] == LEFT)
     def _():
         begin(copies)
-        unpack(e, env_buf)
+        unpack(e, f, role[1], env_buf)
         env = env_buf[...]
         left_sum(env, x, x_buf, sems, y2, w, acc)
         hand_out(acc, scale_of(env), role[1], kept, given)
@@ -226,16 +237,18 @@
     @pl.when(role[0] == RIGHT)
     def _():
         begin(copies)
-        unpack(e, env_buf)
+        unpack(e, f, role[1], env_buf)
         env = env_buf[...]
-        carry_back(env, x, x_buf, sems, natural, cb, cb_out, store_sems)
+        carry_back(env, TILES, x, x_buf, sems, natural, cb, cb_out, store_sems)
         right_sum(y2, cb, acc)
         hand_out(acc, scale_of(env), role[1], kept, given)
         for store in stores:
             store.wait()
 
 
-def last_kernel(role, e1, e2, e3, cb0, cb1, cb2, out, cb, out_buf, narrow, env_buf, factor, sems, side):
+def last_kernel(
+    role, e1, f1, e2, f2, e3, f3, cb0, cb1, cb2, out, cb, out_buf, narrow, env_buf, factor, sems, side
+):
     target_rank, source_rank = env_buf.shape
     block = out_buf.shape[0] // TILES
     lanes = cb.shape[1] // TILES
@@ -255,17 +268,17 @@
             for j in range(TILES):
                 load(source, j).start()
 
-    for group, e in ((1, e1), (2, e2)):
+    for group, e, f in ((1, e1, f1), (2, e2, f2)):
 
         @pl.when(role[0] == group)
         def _():
-            unpack(e, env_buf)
+            unpack(e, f, role[1], env_buf)
 
     @pl.when((role[0] == 0) | (role[0] == 3))
     def _():
-        unpack(e3, env_buf)
-
-    other = jnp.where(role[0] == 1, scale_of(e2[...]), scale_of(e1[...]))
+        unpack(e3, f3, role[1], env_buf)
+
+    other = jnp.where(role[0] == 1, scale_of(e2[...], f2[...]), scale_of(e1[...], f1[...]))
     inner = (role[0] == 1) | (role[0] == 2)
     env = env_buf[...]
     factor[0] = scale_of(env) * jnp.where(inner, other, 1.0) * (1.0 / math.sqrt(source_rank))
@@ -338,7 +351,7 @@
     following = pl.pallas_call(
         next_kernel,
         out_shape=(s_shape, s_shape, HBM(cb_shape.shape, BF16)),
-        in_specs=[place(SMEM), place(VMEM), place(HBM), place(HBM), place(VMEM)],
+        in_specs=[place(SMEM), place(VMEM), place(VMEM), place(HBM), place(HBM), place(VMEM)],
         out_specs=(place(VMEM), place(VMEM), place(HBM)),
         scratch_shapes=[x_buf, cb, w, natural, xt, wide, acc, env_buf, sems, sems, side],
         compiler_params=params,
@@ -347,7 +360,7 @@
     last = pl.pallas_call(
         last_kernel,
         out_shape=jax.ShapeDtypeStruct((target_rank * points, target_rank), BF16),
-        in_specs=[place(SMEM)] + [place(VMEM)] * 3 + [place(HBM)] * 3,
+        in_specs=[place(SMEM)] + [place(VMEM)] * 6 + [place(HBM)] * 3,
         out_specs=place(HBM),
         scratch_shapes=[cb, y_buf, narrow, env_buf, pltpu.SMEM((1,), F32), sems, sems],
         compiler_params=params,
@@ -360,16 +373,15 @@
     chunks, rows, width = kept.shape
     devices = lax.axis_size("mode")
     same_core = [list(range(c, devices, 2)) for c in range(2)]
-    same_chip = [[d, d + 1] for d in range(0, devices, 2)]
-    taken = lax.ppermute(given, "mode", [(d, d ^ 1) for d in range(devices)])
+    neighbour = [(d, d ^ 1) for d in range(devices)]
+    taken = lax.ppermute(given, "mode", neighbour)
     chip = (kept.astype(F32) + taken.astype(F32)).astype(BF16)
     mine = lax.all_to_all(chip, "mode", 0, 0, axis_index_groups=same_core, tiled=True)
     summed = jnp.sum(mine.astype(F32), axis=0).astype(BF16)
     summed = lax.ppermute(summed, "cores", route)
     copies = jnp.broadcast_to(summed[None], (chunks, rows, width))
     whole = lax.all_to_all(copies, "mode", 0, 0, axis_index_groups=same_core, tiled=True)
-    whole = lax.all_gather(whole, "mode", axis_index_groups=same_chip)
-    return whole.reshape(2 * chunks, rows, width)
+    return whole, lax.ppermute(whole, "mode", neighbour)
 
 
 def body(x_cores, y_cores, left_boundary, right_boundary):
@@ -392,10 +404,10 @@
     carried = [cb]
     envs = [exchange(kept, given, [(0, 1), (3, 2)])]
     for position, route in ((1, [(1, 2), (2, 1)]), (2, [(2, 3), (1, 0)])):
-        kept, given, cb = following(role_at(position), envs[-1], left_boundary, x, y2)
+        kept, given, cb = following(role_at(position), *envs[-1], left_boundary, x, y2)
         carried.append(cb)
         envs.append(exchange(kept, given, route))
-    out = last(group.astype(jnp.int32).reshape(1), *envs, *map(in_hbm, carried))
+    out = last(jnp.stack([group, core]).astype(jnp.int32), *sum(envs, ()), *map(in_hbm, carried))
     return out.reshape(1, target_rank, points, target_rank)
 
 

time: 150 us -> 145 us (0.967)
  blocking collectives: 70 us -> 91.6 us
  waiting for transfers between devices: 47.7 us -> 30 us
  starting transfers between devices: 11.5 us -> 3.81 us
    all_to_all x1 -> x3, blocking collectives: 13.8 us -> 41.5 us  [exchange(): lax.all_to_all(copies, 'mode', 0, 0, axis_index_groups=same_core, tiled=T...]
    all_to_all x2 -> x0, waiting for transfers between devices: 21 us -> none  [exchange(): lax.all_to_all(copies, 'mode', 0, 0, axis_index_groups=same_core, tiled=T...]
    all_to_all x2 -> x0, starting transfers between devices: 7.73 us -> none  [exchange(): lax.all_to_all(copies, 'mode', 0, 0, axis_index_groups=same_core, tiled=T...]
    all_gather x3 -> x0, blocking collectives: 5.94 us -> none  [exchange(): whole = lax.all_gather(whole, 'mode', axis_index_groups=same_chip)]
    ppermute x3 -> x6, waiting for transfers between devices: 3.73 us -> 7.54 us  [the longest x3 3.81 us: exchange(): return (whole, lax.ppermute(whole, 'mode', neighbour))]
  transfers between devices with their start and end apart: 8 -> 9, of which waited for: 7 -> 8; matrix products, arithmetic and copies ran while one was open for 0% -> 0% of each run, Pallas kernels for 0% -> 0%
where the time goes in v1:
time: 145 us; the launch traced here: 142 us
  blocking collectives  91.6 us (63%)
  waiting for transfers between devices  30 us (21%)
  Pallas kernels  16.1 us (11%)
  starting transfers between devices  3.81 us (3%)
    all_to_all x3, blocking collectives, exchange(): lax.all_to_all(chip, 'mode', 0, 0, axis_index_groups=same_core, tiled=True)  50.2 us
    all_to_all x3, blocking collectives, exchange(): lax.all_to_all(copies, 'mode', 0, 0, axis_index_groups=same_core, tiled=T...  41.5 us
    ppermute x3, waiting for transfers between devices, exchange(): summed = lax.ppermute(summed, 'cores', route)  22.4 us
    pallas_call x1, Pallas kernels, body(): kept, given, cb, y2 = first(role_at(0), left_boundary, right_boundary, x, y)  8.68 us
    pallas_call x1, Pallas kernels, body(): last(jnp.stack([group, core]).astype(jnp.int32), *sum(envs, ()), *map(in_...  5.7 us
    ppermute x3, waiting for transfers between devices, exchange(): return (whole, lax.ppermute(whole, 'mode', neighbour))  3.81 us
    ppermute x3, waiting for transfers between devices, exchange(): taken = lax.ppermute(given, 'mode', neighbour)  3.73 us
    ppermute x3, starting transfers between devices, exchange(): summed = lax.ppermute(summed, 'cores', route)  3.24 us
  transfers between devices with their start and end apart: 9, of which 8 were waited for; matrix products, arithmetic and copies ran while one was open for 0% of the time, Pallas kernels for 0%

profile of v1, /device:TPU:6, one launch (start us, length us, event | category | flops | bytes accessed | tf_op | source)
XLA Modules:
  0.0 142.4 jit_solution(12917142150803217575)
XLA Ops:
  0.0 0.1 pad_add_fusion.1.role
  0.1 8.7 %first_step.1 = (bf16[32,16,128]{2,1,0:T(8,128)(2,1)S(1)}, bf16[32,16,128]{2,1,0:T(8,128)(2,1)S(1)}, bf16[512,4096]{1,0:T(8,128)(2,1)}, bf16[256,4096]{1,0:T(8,128)(2,1)S(1)}) custom-call(s32[2]{0:T(128)S(1)} %pad_add_fusion.1.role, bf16[256,512]{1,0:T(8,128)(2,1)} %lb.5, bf16[256,512]{1,0:T(8,128)(2,1)} %rb.1, bf16[8192,512]{1,0:T(8,128)(2,1)} %bitcast.8, ...), custom_call_target="tpu_custom_call" | custom-call | tf_op jit(solution)/shard_map/first_step/pallas_call | solution.py:403
  8.8 0.1 collective-permute-start
  8.9 1.3 collective-permute-done
  10.2 22.1 %all_to_all.30 = bf16[32,16,128]{2,1,0:T(8,128)(2,1)S(1)} all-to-all(bf16[32,16,128]{2,1,0:T(8,128)(2,1)S(1)} %add_convert_fusion.2), channel_id=1, replica_groups={{0,2,4,6,8,10,12,14,16,18,20,22,24,26,28,30,32,34,36,38,40,42,44,46,48,..., dimensions={0} | all-to-all | bytes 262144 | tf_op jit(solution)/shard_map/all_to_all | solution.py:379
  32.4 1.3 collective-permute-start.1
  33.7 1.3 collective-permute-done.1
  35.0 13.8 %all_to_all.31.e.e1 = bf16[32,16,128]{2,1,0:T(8,128)(2,1)S(1)} all-to-all(bf16[32,16,128]{2,1,0:T(8,128)(2,1)S(1)} %broadcast_in_dim.6), channel_id=1, replica_groups={{0,2,4,6,8,10,12,14,16,18,20,22,24,26,28,30,32,34,36,38,40,42,44,46,48,..., dimensions={0} | all-to-all | bytes 262144 | tf_op jit(solution)/shard_map/all_to_all | solution.py:383
  48.8 0.0 collective-permute-start.2
  48.8 0.1 pad_add_fusion.2.role
  48.9 1.3 collective-permute-done.2.f.f1
  50.2 0.8 next_step.2
  51.0 0.2 collective-permute-start.3
  51.2 1.2 collective-permute-done.3
  52.4 14.0 %all_to_all.32 = bf16[32,16,128]{2,1,0:T(8,128)(2,1)S(1)} all-to-all(bf16[32,16,128]{2,1,0:T(8,128)(2,1)S(1)} %add_convert_fusion.1), channel_id=1, replica_groups={{0,2,4,6,8,10,12,14,16,18,20,22,24,26,28,30,32,34,36,38,40,42,44,46,48,..., dimensions={0} | all-to-all | bytes 262144 | tf_op jit(solution)/shard_map/all_to_all | solution.py:379
  66.5 0.7 collective-permute-start.4
  67.2 0.0 collective-permute-done.4
  67.2 13.8 %all_to_all.33.e.e2 = bf16[32,16,128]{2,1,0:T(8,128)(2,1)S(1)} all-to-all(bf16[32,16,128]{2,1,0:T(8,128)(2,1)S(1)} %broadcast_in_dim.7), channel_id=1, replica_groups={{0,2,4,6,8,10,12,14,16,18,20,22,24,26,28,30,32,34,36,38,40,42,44,46,48,..., dimensions={0} | all-to-all | bytes 262144 | tf_op jit(solution)/shard_map/all_to_all | solution.py:383
  81.1 0.0 collective-permute-start.5
  81.1 0.1 pad_add_fusion.3.role
  81.1 1.3 collective-permute-done.5.f.f2
  82.4 1.0 next_step.3
  83.4 0.2 collective-permute-start.6
  83.6 1.2 collective-permute-done.6
  84.8 14.0 %all_to_all.34 = bf16[32,16,128]{2,1,0:T(8,128)(2,1)S(1)} all-to-all(bf16[32,16,128]{2,1,0:T(8,128)(2,1)S(1)} %add_convert_fusion), channel_id=1, replica_groups={{0,2,4,6,8,10,12,14,16,18,20,22,24,26,28,30,32,34,36,38,40,42,44,46,48,..., dimensions={0} | all-to-all | bytes 262144 | tf_op jit(solution)/shard_map/all_to_all | solution.py:379
  98.9 1.3 collective-permute-start.7
  100.2 21.1 %collective-permute-done.7 = bf16[16,128]{1,0:T(8,128)(2,1)S(1)} collective-permute-done((bf16[16,128]{1,0:T(8,128)(2,1)S(1)}, bf16[16,128]{1,0:T(8,128)(2,1)S(1)}, u32[]{:S(2)}, u32[]{:S(2)}) %collective-permute-start.7) | collective-permute-done | bytes 4128 | tf_op jit(solution)/shard_map/ppermute | solution.py:381
  121.3 13.8 %all_to_all.35.e3 = bf16[32,16,128]{2,1,0:T(8,128)(2,1)S(1)} all-to-all(bf16[32,16,128]{2,1,0:T(8,128)(2,1)S(1)} %broadcast_in_dim.8), channel_id=1, replica_groups={{0,2,4,6,8,10,12,14,16,18,20,22,24,26,28,30,32,34,36,38,40,42,44,46,48,..., dimensions={0} | all-to-all | bytes 262144 | tf_op jit(solution)/shard_map/all_to_all | solution.py:383
  135.2 0.0 collective-permute-start.8
  135.2 0.1 pad_add_fusion.role
  135.2 1.3 collective-permute-done.8.f3
  136.5 5.7 %projection.1 = bf16[4096,256]{1,0:T(8,128)(2,1)} custom-call(s32[2]{0:T(128)S(1)} %pad_add_fusion.role, bf16[32,16,128]{2,1,0:T(8,128)(2,1)S(1)} %all_to_all.31.e.e1, bf16[32,16,128]{2,1,0:T(8,128)(2,1)S(1)} %collective-permute-done.2.f.f1, bf16[32,16,128]{2,1,0:T(8,128)(2,1)S(1)} %all_to_all.33.e.e2, bf16[32,16,128]{2,1,0:T(8,128)(2,1)S(1)} %collective-permute-done.5.f.f2, ...), custom_call_target="tpu_custom_call" | custom-call | tf_op jit(solution)/shard_map/projection/pallas_call | solution.py:410
  (9 shorter events, 0.3 us)
Async XLA Ops:
  8.8 1.4 %collective-permute-start = (bf16[32,16,128]{2,1,0:T(8,128)(2,1)S(1)}, bf16[32,16,128]{2,1,0:T(8,128)(2,1)S(1)}, u32[]{:S(2)}, u32[]{:S(2)}) collective-permute-start(bf16[32,16,128]{2,1,0:T(8,128)(2,1)S(1)} %get-tuple-element.16), channel_id=1, source_target_pairs={{0,1},{1,0},{2,3},{3,2},{4,5},{5,4},{6,7},{7,6},{8,9},{9,8},{10,11... | collective-permute-start | bytes 393224 | tf_op jit(solution)/shard_map/ppermute | solution.py:377
  32.4 2.6 %collective-permute-start.1 = (bf16[16,128]{1,0:T(8,128)(2,1)S(1)}, bf16[16,128]{1,0:T(8,128)(2,1)S(1)}, u32[]{:S(2)}, u32[]{:S(2)}) collective-permute-start(bf16[16,128]{1,0:T(8,128)(2,1)S(1)} %reduce_sum.36), channel_id=1, source_target_pairs={{0,64},{192,128},{1,65},{193,129},{2,66},{194,130},{3,67},{195,131... | collective-permute-start | bytes 12296 | tf_op jit(solution)/shard_map/ppermute | solution.py:381
  48.8 1.3 collective-permute-start.2
  51.0 1.4 %collective-permute-start.3 = (bf16[32,16,128]{2,1,0:T(8,128)(2,1)S(1)}, bf16[32,16,128]{2,1,0:T(8,128)(2,1)S(1)}, u32[]{:S(2)}, u32[]{:S(2)}) collective-permute-start(bf16[32,16,128]{2,1,0:T(8,128)(2,1)S(1)} %get-tuple-element.19), channel_id=1, source_target_pairs={{0,1},{1,0},{2,3},{3,2},{4,5},{5,4},{6,7},{7,6},{8,9},{9,8},{10,11... | collective-permute-start | bytes 393224 | tf_op jit(solution)/shard_map/ppermute | solution.py:377
  66.5 0.7 collective-permute-start.4
  81.1 1.3 collective-permute-start.5
  83.4 1.4 %collective-permute-start.6 = (bf16[32,16,128]{2,1,0:T(8,128)(2,1)S(1)}, bf16[32,16,128]{2,1,0:T(8,128)(2,1)S(1)}, u32[]{:S(2)}, u32[]{:S(2)}) collective-permute-start(bf16[32,16,128]{2,1,0:T(8,128)(2,1)S(1)} %get-tuple-element.21), channel_id=1, source_target_pairs={{0,1},{1,0},{2,3},{3,2},{4,5},{5,4},{6,7},{7,6},{8,9},{9,8},{10,11... | collective-permute-start | bytes 393224 | tf_op jit(solution)/shard_map/ppermute | solution.py:377
  98.9 22.4 %collective-permute-start.7 = (bf16[16,128]{1,0:T(8,128)(2,1)S(1)}, bf16[16,128]{1,0:T(8,128)(2,1)S(1)}, u32[]{:S(2)}, u32[]{:S(2)}) collective-permute-start(bf16[16,128]{1,0:T(8,128)(2,1)S(1)} %reduce_sum.38), channel_id=1, source_target_pairs={{128,192},{64,0},{129,193},{65,1},{130,194},{66,2},{131,195},{67,3... | collective-permute-start | bytes 12296 | tf_op jit(solution)/shard_map/ppermute | solution.py:381
  135.2 1.3 collective-permute-start.8

commit v2 on v1

--- a/solution.py
+++ b/solution.py
@@ -26,7 +26,7 @@
     chunks, rows, width = own.shape
     lanes = env_ref.shape[1] // width
     half = env_ref.shape[0] // 2
-    for ref, owner in ((own, core), (others, 1 - core)):
+    for ref, owner in ((own, 1 - core), (others, core)):
         for j in range(chunks):
             r, k = j // lanes, j % lanes
             start = pl.multiple_of(owner * half + rows * r, rows)
@@ -378,7 +378,10 @@
     chip = (kept.astype(F32) + taken.astype(F32)).astype(BF16)
     mine = lax.all_to_all(chip, "mode", 0, 0, axis_index_groups=same_core, tiled=True)
     summed = jnp.sum(mine.astype(F32), axis=0).astype(BF16)
-    summed = lax.ppermute(summed, "cores", route)
+    hops = [
+        (source * devices + d, target * devices + (d ^ 1)) for source, target in route for d in range(devices)
+    ]
+    summed = lax.ppermute(summed, ("cores", "mode"), hops)
     copies = jnp.broadcast_to(summed[None], (chunks, rows, width))
     whole = lax.all_to_all(copies, "mode", 0, 0, axis_index_groups=same_core, tiled=True)
     return whole, lax.ppermute(whole, "mode", neighbour)

time: 145 us -> 143 us (0.986)
  waiting for transfers between devices: 30 us -> 26.5 us
  blocking collectives: 91.6 us -> 93.2 us
    ppermute x3, waiting for transfers between devices: 22.4 us -> 19.1 us  [exchange(): summed = lax.ppermute(summed, ('cores', 'mode'), hops)]
    all_to_all x3, blocking collectives: 41.5 us -> 43.1 us  [exchange(): lax.all_to_all(copies, 'mode', 0, 0, axis_index_groups=same_core, tiled=T...]
where the time goes in v2:
time: 143 us; the launch traced here: 141 us
  blocking collectives  93.2 us (65%)
  waiting for transfers between devices  26.5 us (19%)
  Pallas kernels  16.1 us (11%)
  starting transfers between devices  3.93 us (3%)
    all_to_all x3, blocking collectives, exchange(): lax.all_to_all(chip, 'mode', 0, 0, axis_index_groups=same_core, tiled=True)  50.2 us
    all_to_all x3, blocking collectives, exchange(): lax.all_to_all(copies, 'mode', 0, 0, axis_index_groups=same_core, tiled=T...  43.1 us
    ppermute x3, waiting for transfers between devices, exchange(): summed = lax.ppermute(summed, ('cores', 'mode'), hops)  19.1 us
    pallas_call x1, Pallas kernels, body(): kept, given, cb, y2 = first(role_at(0), left_boundary, right_boundary, x, y)  8.68 us
    pallas_call x1, Pallas kernels, body(): last(jnp.stack([group, core]).astype(jnp.int32), *sum(envs, ()), *map(in_...  5.7 us
    ppermute x3, waiting for transfers between devices, exchange(): taken = lax.ppermute(given, 'mode', neighbour)  3.73 us
    ppermute x3, waiting for transfers between devices, exchange(): return (whole, lax.ppermute(whole, 'mode', neighbour))  3.7 us
    ppermute x3, starting transfers between devices, exchange(): summed = lax.ppermute(summed, ('cores', 'mode'), hops)  3.24 us
  transfers between devices with their start and end apart: 9, of which 8 were waited for; matrix products, arithmetic and copies ran while one was open for 0% of the time, Pallas kernels for 0%

profile of v2, /device:TPU:6, one launch (start us, length us, event | category | flops | bytes accessed | tf_op | source)
XLA Modules:
  0.0 140.6 jit_solution(1374914760572817709)
XLA Ops:
  0.0 0.1 pad_add_fusion.1.role
  0.1 8.7 %first_step.1 = (bf16[32,16,128]{2,1,0:T(8,128)(2,1)S(1)}, bf16[32,16,128]{2,1,0:T(8,128)(2,1)S(1)}, bf16[512,4096]{1,0:T(8,128)(2,1)}, bf16[256,4096]{1,0:T(8,128)(2,1)S(1)}) custom-call(s32[2]{0:T(128)S(1)} %pad_add_fusion.1.role, bf16[256,512]{1,0:T(8,128)(2,1)} %lb.5, bf16[256,512]{1,0:T(8,128)(2,1)} %rb.1, bf16[8192,512]{1,0:T(8,128)(2,1)} %bitcast.8, ...), custom_call_target="tpu_custom_call" | custom-call | tf_op jit(solution)/shard_map/first_step/pallas_call | solution.py:406
  8.8 0.1 collective-permute-start
  8.9 1.3 collective-permute-done
  10.2 22.1 %all_to_all.30 = bf16[32,16,128]{2,1,0:T(8,128)(2,1)S(1)} all-to-all(bf16[32,16,128]{2,1,0:T(8,128)(2,1)S(1)} %add_convert_fusion.2), channel_id=1, replica_groups={{0,2,4,6,8,10,12,14,16,18,20,22,24,26,28,30,32,34,36,38,40,42,44,46,48,..., dimensions={0} | all-to-all | bytes 262144 | tf_op jit(solution)/shard_map/all_to_all | solution.py:379
  32.4 1.3 collective-permute-start.1
  33.7 1.3 collective-permute-done.1
  35.0 13.8 %all_to_all.31.e.e1 = bf16[32,16,128]{2,1,0:T(8,128)(2,1)S(1)} all-to-all(bf16[32,16,128]{2,1,0:T(8,128)(2,1)S(1)} %broadcast_in_dim.6), channel_id=1, replica_groups={{0,2,4,6,8,10,12,14,16,18,20,22,24,26,28,30,32,34,36,38,40,42,44,46,48,..., dimensions={0} | all-to-all | bytes 262144 | tf_op jit(solution)/shard_map/all_to_all | solution.py:386
  48.8 0.0 collective-permute-start.2
  48.8 0.1 pad_add_fusion.2.role
  48.9 1.3 collective-permute-done.2.f.f1
  50.2 0.8 next_step.2
  51.0 0.2 collective-permute-start.3
  51.2 1.2 collective-permute-done.3
  52.4 14.0 %all_to_all.32 = bf16[32,16,128]{2,1,0:T(8,128)(2,1)S(1)} all-to-all(bf16[32,16,128]{2,1,0:T(8,128)(2,1)S(1)} %add_convert_fusion.1), channel_id=1, replica_groups={{0,2,4,6,8,10,12,14,16,18,20,22,24,26,28,30,32,34,36,38,40,42,44,46,48,..., dimensions={0} | all-to-all | bytes 262144 | tf_op jit(solution)/shard_map/all_to_all | solution.py:379
  66.5 0.7 collective-permute-start.4
  67.2 0.0 collective-permute-done.4
  67.2 13.8 %all_to_all.33.e.e2 = bf16[32,16,128]{2,1,0:T(8,128)(2,1)S(1)} all-to-all(bf16[32,16,128]{2,1,0:T(8,128)(2,1)S(1)} %broadcast_in_dim.7), channel_id=1, replica_groups={{0,2,4,6,8,10,12,14,16,18,20,22,24,26,28,30,32,34,36,38,40,42,44,46,48,..., dimensions={0} | all-to-all | bytes 262144 | tf_op jit(solution)/shard_map/all_to_all | solution.py:386
  81.1 0.0 collective-permute-start.5
  81.1 0.1 pad_add_fusion.3.role
  81.1 1.3 collective-permute-done.5.f.f2
  82.4 1.0 next_step.3
  83.4 0.2 collective-permute-start.6
  83.6 1.2 collective-permute-done.6
  84.8 14.0 %all_to_all.34 = bf16[32,16,128]{2,1,0:T(8,128)(2,1)S(1)} all-to-all(bf16[32,16,128]{2,1,0:T(8,128)(2,1)S(1)} %add_convert_fusion), channel_id=1, replica_groups={{0,2,4,6,8,10,12,14,16,18,20,22,24,26,28,30,32,34,36,38,40,42,44,46,48,..., dimensions={0} | all-to-all | bytes 262144 | tf_op jit(solution)/shard_map/all_to_all | solution.py:379
  98.9 1.3 collective-permute-start.7
  100.2 17.7 %collective-permute-done.7 = bf16[16,128]{1,0:T(8,128)(2,1)S(1)} collective-permute-done((bf16[16,128]{1,0:T(8,128)(2,1)S(1)}, bf16[16,128]{1,0:T(8,128)(2,1)S(1)}, u32[]{:S(2)}, u32[]{:S(2)}) %collective-permute-start.7) | collective-permute-done | bytes 4128 | tf_op jit(solution)/shard_map/ppermute | solution.py:384
  118.0 15.4 %all_to_all.35.e3 = bf16[32,16,128]{2,1,0:T(8,128)(2,1)S(1)} all-to-all(bf16[32,16,128]{2,1,0:T(8,128)(2,1)S(1)} %broadcast_in_dim.8), channel_id=1, replica_groups={{0,2,4,6,8,10,12,14,16,18,20,22,24,26,28,30,32,34,36,38,40,42,44,46,48,..., dimensions={0} | all-to-all | bytes 262144 | tf_op jit(solution)/shard_map/all_to_all | solution.py:386
  133.4 0.1 collective-permute-start.8
  133.5 0.1 pad_add_fusion.role
  133.6 1.2 collective-permute-done.8.f3
  134.7 5.7 %projection.1 = bf16[4096,256]{1,0:T(8,128)(2,1)} custom-call(s32[2]{0:T(128)S(1)} %pad_add_fusion.role, bf16[32,16,128]{2,1,0:T(8,128)(2,1)S(1)} %all_to_all.31.e.e1, bf16[32,16,128]{2,1,0:T(8,128)(2,1)S(1)} %collective-permute-done.2.f.f1, bf16[32,16,128]{2,1,0:T(8,128)(2,1)S(1)} %all_to_all.33.e.e2, bf16[32,16,128]{2,1,0:T(8,128)(2,1)S(1)} %collective-permute-done.5.f.f2, ...), custom_call_target="tpu_custom_call" | custom-call | tf_op jit(solution)/shard_map/projection/pallas_call | solution.py:413
  (9 shorter events, 0.3 us)
Async XLA Ops:
  8.8 1.4 %collective-permute-start = (bf16[32,16,128]{2,1,0:T(8,128)(2,1)S(1)}, bf16[32,16,128]{2,1,0:T(8,128)(2,1)S(1)}, u32[]{:S(2)}, u32[]{:S(2)}) collective-permute-start(bf16[32,16,128]{2,1,0:T(8,128)(2,1)S(1)} %get-tuple-element.16), channel_id=1, source_target_pairs={{0,1},{1,0},{2,3},{3,2},{4,5},{5,4},{6,7},{7,6},{8,9},{9,8},{10,11... | collective-permute-start | bytes 393224 | tf_op jit(solution)/shard_map/ppermute | solution.py:377
  32.4 2.6 %collective-permute-start.1 = (bf16[16,128]{1,0:T(8,128)(2,1)S(1)}, bf16[16,128]{1,0:T(8,128)(2,1)S(1)}, u32[]{:S(2)}, u32[]{:S(2)}) collective-permute-start(bf16[16,128]{1,0:T(8,128)(2,1)S(1)} %reduce_sum.36), channel_id=1, source_target_pairs={{0,65},{1,64},{2,67},{3,66},{4,69},{5,68},{6,71},{7,70},{8,73},{9,... | collective-permute-start | bytes 12296 | tf_op jit(solution)/shard_map/ppermute | solution.py:384
  48.8 1.3 collective-permute-start.2
  51.0 1.4 %collective-permute-start.3 = (bf16[32,16,128]{2,1,0:T(8,128)(2,1)S(1)}, bf16[32,16,128]{2,1,0:T(8,128)(2,1)S(1)}, u32[]{:S(2)}, u32[]{:S(2)}) collective-permute-start(bf16[32,16,128]{2,1,0:T(8,128)(2,1)S(1)} %get-tuple-element.19), channel_id=1, source_target_pairs={{0,1},{1,0},{2,3},{3,2},{4,5},{5,4},{6,7},{7,6},{8,9},{9,8},{10,11... | collective-permute-start | bytes 393224 | tf_op jit(solution)/shard_map/ppermute | solution.py:377
  66.5 0.7 collective-permute-start.4
  81.1 1.3 collective-permute-start.5
  83.4 1.4 %collective-permute-start.6 = (bf16[32,16,128]{2,1,0:T(8,128)(2,1)S(1)}, bf16[32,16,128]{2,1,0:T(8,128)(2,1)S(1)}, u32[]{:S(2)}, u32[]{:S(2)}) collective-permute-start(bf16[32,16,128]{2,1,0:T(8,128)(2,1)S(1)} %get-tuple-element.21), channel_id=1, source_target_pairs={{0,1},{1,0},{2,3},{3,2},{4,5},{5,4},{6,7},{7,6},{8,9},{9,8},{10,11... | collective-permute-start | bytes 393224 | tf_op jit(solution)/shard_map/ppermute | solution.py:377
  98.9 19.0 %collective-permute-start.7 = (bf16[16,128]{1,0:T(8,128)(2,1)S(1)}, bf16[16,128]{1,0:T(8,128)(2,1)S(1)}, u32[]{:S(2)}, u32[]{:S(2)}) collective-permute-start(bf16[16,128]{1,0:T(8,128)(2,1)S(1)} %reduce_sum.38), channel_id=1, source_target_pairs={{128,193},{129,192},{130,195},{131,194},{132,197},{133,196},{134,1... | collective-permute-start | bytes 12296 | tf_op jit(solution)/shard_map/ppermute | solution.py:384
  133.4 1.3 collective-permute-start.8

commit v3 on v2

--- a/solution.py
+++ b/solution.py
@@ -11,7 +11,7 @@
 EPSILON = 1e-06
 TILES = 8
 PARTS = 2
-WINDOW = 3
+WINDOW = 4
 LANES = 128
 VMEM_LIMIT = 36 * 1024 * 1024
 BF16 = jnp.bfloat16
@@ -109,20 +109,23 @@
     ranks = cb.shape[0] // TILES
     turned = env.T
 
-    @pl.loop(0, TILES)
-    def _(t):
-        tile_copy(x_ref, x, sems, t).wait()
-
-        if window < TILES:
-
-            @pl.when(t + window < TILES)
-            def _():
-                tile_copy(x_ref, x, sems, t + window).start()
-
-        value = jnp.dot(x[block_of(t, rows), :], turned, preferred_element_type=F32)
-        natural[...] = value.astype(BF16)
-        cb[block_of(t, ranks), :] = natural[...].reshape(ranks, cb.shape[1])
-        tile_copy(cb, cb_out, store_sems, t).start()
+    @pl.loop(0, TILES // 2)
+    def _(pair):
+        for u in range(2):
+            t = pair * 2 + u
+            tile_copy(x_ref, x, sems, t).wait()
+            if window < TILES:
+
+                @pl.when(t + window < TILES)
+                def _():
+                    tile_copy(x_ref, x, sems, t + window).start()
+
+        for u in range(2):
+            value = jnp.dot(x[block_of(pair * 2 + u, rows), :], turned, preferred_element_type=F32)
+            natural[u] = value.astype(BF16)
+            cb[block_of(pair * 2 + u, ranks), :] = natural[u].reshape(ranks, cb.shape[1])
+        for u in range(2):
+            tile_copy(cb, cb_out, store_sems, pair * 2 + u).start()
 
 
 def right_sum(y2, cb, acc):
@@ -330,7 +333,7 @@
     cb = pltpu.VMEM(cb_shape.shape, BF16)
     y_buf = pltpu.VMEM((target_rank * points, target_rank), BF16)
     w = pltpu.VMEM(cb_shape.shape, BF16)
-    natural = pltpu.VMEM((rows // TILES, target_rank), BF16)
+    natural = pltpu.VMEM((2, rows // TILES, target_rank), BF16)
     xt = pltpu.VMEM((source_rank, points * source_rank), BF16)
     wide = pltpu.VMEM((target_rank, points * source_rank), BF16)
     narrow = pltpu.VMEM((target_rank, flat), BF16)

time: 143 us -> 143 us (level)
  no operation moved by 1% of the time
where the time goes in v3:
time: 143 us; the launch traced here: 140 us
  blocking collectives  93.2 us (65%)
  waiting for transfers between devices  26.5 us (19%)
  Pallas kernels  15.9 us (11%)
  starting transfers between devices  3.93 us (3%)
    all_to_all x3, blocking collectives, exchange(): lax.all_to_all(chip, 'mode', 0, 0, axis_index_groups=same_core, tiled=True)  50.2 us
    all_to_all x3, blocking collectives, exchange(): lax.all_to_all(copies, 'mode', 0, 0, axis_index_groups=same_core, tiled=T...  43.1 us
    ppermute x3, waiting for transfers between devices, exchange(): summed = lax.ppermute(summed, ('cores', 'mode'), hops)  19 us
    pallas_call x1, Pallas kernels, body(): kept, given, cb, y2 = first(role_at(0), left_boundary, right_boundary, x, y)  8.47 us
    pallas_call x1, Pallas kernels, body(): last(jnp.stack([group, core]).astype(jnp.int32), *sum(envs, ()), *map(in_...  5.7 us
    ppermute x3, waiting for transfers between devices, exchange(): taken = lax.ppermute(given, 'mode', neighbour)  3.73 us
    ppermute x3, waiting for transfers between devices, exchange(): return (whole, lax.ppermute(whole, 'mode', neighbour))  3.7 us
    ppermute x3, starting transfers between devices, exchange(): summed = lax.ppermute(summed, ('cores', 'mode'), hops)  3.24 us
  transfers between devices with their start and end apart: 9, of which 8 were waited for; matrix products, arithmetic and copies ran while one was open for 0% of the time, Pallas kernels for 0%

profile of v3, /device:TPU:6, one launch (start us, length us, event | category | flops | bytes accessed | tf_op | source)
XLA Modules:
  0.0 140.4 jit_solution(1653792077594199778)
XLA Ops:
  0.0 0.1 pad_add_fusion.1.role
  0.1 8.5 %first_step.1 = (bf16[32,16,128]{2,1,0:T(8,128)(2,1)S(1)}, bf16[32,16,128]{2,1,0:T(8,128)(2,1)S(1)}, bf16[512,4096]{1,0:T(8,128)(2,1)}, bf16[256,4096]{1,0:T(8,128)(2,1)S(1)}) custom-call(s32[2]{0:T(128)S(1)} %pad_add_fusion.1.role, bf16[256,512]{1,0:T(8,128)(2,1)} %lb.5, bf16[256,512]{1,0:T(8,128)(2,1)} %rb.1, bf16[8192,512]{1,0:T(8,128)(2,1)} %bitcast.8, ...), custom_call_target="tpu_custom_call" | custom-call | tf_op jit(solution)/shard_map/first_step/pallas_call | solution.py:409
  8.6 0.1 collective-permute-start
  8.7 1.3 collective-permute-done
  10.0 22.1 %all_to_all.30 = bf16[32,16,128]{2,1,0:T(8,128)(2,1)S(1)} all-to-all(bf16[32,16,128]{2,1,0:T(8,128)(2,1)S(1)} %add_convert_fusion.2), channel_id=1, replica_groups={{0,2,4,6,8,10,12,14,16,18,20,22,24,26,28,30,32,34,36,38,40,42,44,46,48,..., dimensions={0} | all-to-all | bytes 262144 | tf_op jit(solution)/shard_map/all_to_all | solution.py:382
  32.2 1.3 collective-permute-start.1
  33.5 1.3 collective-permute-done.1
  34.8 13.8 %all_to_all.31.e.e1 = bf16[32,16,128]{2,1,0:T(8,128)(2,1)S(1)} all-to-all(bf16[32,16,128]{2,1,0:T(8,128)(2,1)S(1)} %broadcast_in_dim.6), channel_id=1, replica_groups={{0,2,4,6,8,10,12,14,16,18,20,22,24,26,28,30,32,34,36,38,40,42,44,46,48,..., dimensions={0} | all-to-all | bytes 262144 | tf_op jit(solution)/shard_map/all_to_all | solution.py:389
  48.6 0.0 collective-permute-start.2
  48.6 0.1 pad_add_fusion.2.role
  48.7 1.3 collective-permute-done.2.f.f1
  50.0 0.8 next_step.2
  50.7 0.2 collective-permute-start.3
  51.0 1.2 collective-permute-done.3
  52.2 14.0 %all_to_all.32 = bf16[32,16,128]{2,1,0:T(8,128)(2,1)S(1)} all-to-all(bf16[32,16,128]{2,1,0:T(8,128)(2,1)S(1)} %add_convert_fusion.1), channel_id=1, replica_groups={{0,2,4,6,8,10,12,14,16,18,20,22,24,26,28,30,32,34,36,38,40,42,44,46,48,..., dimensions={0} | all-to-all | bytes 262144 | tf_op jit(solution)/shard_map/all_to_all | solution.py:382
  66.3 0.7 collective-permute-start.4
  67.0 0.0 collective-permute-done.4
  67.0 13.8 %all_to_all.33.e.e2 = bf16[32,16,128]{2,1,0:T(8,128)(2,1)S(1)} all-to-all(bf16[32,16,128]{2,1,0:T(8,128)(2,1)S(1)} %broadcast_in_dim.7), channel_id=1, replica_groups={{0,2,4,6,8,10,12,14,16,18,20,22,24,26,28,30,32,34,36,38,40,42,44,46,48,..., dimensions={0} | all-to-all | bytes 262144 | tf_op jit(solution)/shard_map/all_to_all | solution.py:389
  80.8 0.0 collective-permute-start.5
  80.8 0.1 pad_add_fusion.3.role
  80.9 1.3 collective-permute-done.5.f.f2
  82.2 1.0 next_step.3
  83.1 0.2 collective-permute-start.6
  83.4 1.2 collective-permute-done.6
  84.6 14.0 %all_to_all.34 = bf16[32,16,128]{2,1,0:T(8,128)(2,1)S(1)} all-to-all(bf16[32,16,128]{2,1,0:T(8,128)(2,1)S(1)} %add_convert_fusion), channel_id=1, replica_groups={{0,2,4,6,8,10,12,14,16,18,20,22,24,26,28,30,32,34,36,38,40,42,44,46,48,..., dimensions={0} | all-to-all | bytes 262144 | tf_op jit(solution)/shard_map/all_to_all | solution.py:382
  98.7 1.3 collective-permute-start.7
  100.0 17.7 %collective-permute-done.7 = bf16[16,128]{1,0:T(8,128)(2,1)S(1)} collective-permute-done((bf16[16,128]{1,0:T(8,128)(2,1)S(1)}, bf16[16,128]{1,0:T(8,128)(2,1)S(1)}, u32[]{:S(2)}, u32[]{:S(2)}) %collective-permute-start.7) | collective-permute-done | bytes 4128 | tf_op jit(solution)/shard_map/ppermute | solution.py:387
  117.7 15.4 %all_to_all.35.e3 = bf16[32,16,128]{2,1,0:T(8,128)(2,1)S(1)} all-to-all(bf16[32,16,128]{2,1,0:T(8,128)(2,1)S(1)} %broadcast_in_dim.8), channel_id=1, replica_groups={{0,2,4,6,8,10,12,14,16,18,20,22,24,26,28,30,32,34,36,38,40,42,44,46,48,..., dimensions={0} | all-to-all | bytes 262144 | tf_op jit(solution)/shard_map/all_to_all | solution.py:389
  133.1 0.1 collective-permute-start.8
  133.3 0.1 pad_add_fusion.role
  133.3 1.2 collective-permute-done.8.f3
  134.5 5.7 %projection.1 = bf16[4096,256]{1,0:T(8,128)(2,1)} custom-call(s32[2]{0:T(128)S(1)} %pad_add_fusion.role, bf16[32,16,128]{2,1,0:T(8,128)(2,1)S(1)} %all_to_all.31.e.e1, bf16[32,16,128]{2,1,0:T(8,128)(2,1)S(1)} %collective-permute-done.2.f.f1, bf16[32,16,128]{2,1,0:T(8,128)(2,1)S(1)} %all_to_all.33.e.e2, bf16[32,16,128]{2,1,0:T(8,128)(2,1)S(1)} %collective-permute-done.5.f.f2, ...), custom_call_target="tpu_custom_call" | custom-call | tf_op jit(solution)/shard_map/projection/pallas_call | solution.py:416
  (9 shorter events, 0.3 us)
Async XLA Ops:
  8.6 1.4 %collective-permute-start = (bf16[32,16,128]{2,1,0:T(8,128)(2,1)S(1)}, bf16[32,16,128]{2,1,0:T(8,128)(2,1)S(1)}, u32[]{:S(2)}, u32[]{:S(2)}) collective-permute-start(bf16[32,16,128]{2,1,0:T(8,128)(2,1)S(1)} %get-tuple-element.16), channel_id=1, source_target_pairs={{0,1},{1,0},{2,3},{3,2},{4,5},{5,4},{6,7},{7,6},{8,9},{9,8},{10,11... | collective-permute-start | bytes 393224 | tf_op jit(solution)/shard_map/ppermute | solution.py:380
  32.2 2.6 %collective-permute-start.1 = (bf16[16,128]{1,0:T(8,128)(2,1)S(1)}, bf16[16,128]{1,0:T(8,128)(2,1)S(1)}, u32[]{:S(2)}, u32[]{:S(2)}) collective-permute-start(bf16[16,128]{1,0:T(8,128)(2,1)S(1)} %reduce_sum.36), channel_id=1, source_target_pairs={{0,65},{1,64},{2,67},{3,66},{4,69},{5,68},{6,71},{7,70},{8,73},{9,... | collective-permute-start | bytes 12296 | tf_op jit(solution)/shard_map/ppermute | solution.py:387
  48.6 1.3 collective-permute-start.2
  50.7 1.4 %collective-permute-start.3 = (bf16[32,16,128]{2,1,0:T(8,128)(2,1)S(1)}, bf16[32,16,128]{2,1,0:T(8,128)(2,1)S(1)}, u32[]{:S(2)}, u32[]{:S(2)}) collective-permute-start(bf16[32,16,128]{2,1,0:T(8,128)(2,1)S(1)} %get-tuple-element.19), channel_id=1, source_target_pairs={{0,1},{1,0},{2,3},{3,2},{4,5},{5,4},{6,7},{7,6},{8,9},{9,8},{10,11... | collective-permute-start | bytes 393224 | tf_op jit(solution)/shard_map/ppermute | solution.py:380
  66.3 0.7 collective-permute-start.4
  80.8 1.3 collective-permute-start.5
  83.1 1.4 %collective-permute-start.6 = (bf16[32,16,128]{2,1,0:T(8,128)(2,1)S(1)}, bf16[32,16,128]{2,1,0:T(8,128)(2,1)S(1)}, u32[]{:S(2)}, u32[]{:S(2)}) collective-permute-start(bf16[32,16,128]{2,1,0:T(8,128)(2,1)S(1)} %get-tuple-element.21), channel_id=1, source_target_pairs={{0,1},{1,0},{2,3},{3,2},{4,5},{5,4},{6,7},{7,6},{8,9},{9,8},{10,11... | collective-permute-start | bytes 393224 | tf_op jit(solution)/shard_map/ppermute | solution.py:380
  98.7 19.0 %collective-permute-start.7 = (bf16[16,128]{1,0:T(8,128)(2,1)S(1)}, bf16[16,128]{1,0:T(8,128)(2,1)S(1)}, u32[]{:S(2)}, u32[]{:S(2)}) collective-permute-start(bf16[16,128]{1,0:T(8,128)(2,1)S(1)} %reduce_sum.38), channel_id=1, source_target_pairs={{128,193},{129,192},{130,195},{131,194},{132,197},{133,196},{134,1... | collective-permute-start | bytes 12296 | tf_op jit(solution)/shard_map/ppermute | solution.py:387
  133.1 1.3 collective-permute-start.8
